TPU v7x, 512 devices: a whole 4x4x16 slice. The times are simulated.
512 devices in a mesh: leaf: 32 (over z, core), frow: 4 (over x), fcol: 4 (over y).
Axes of the slice: x: 4, y: 4, z: 16, core: 2. Of those that a mesh axis runs over, the one named last changes fastest.
Arguments:
- child_update: float32 [32, 3584, 3584], P('leaf', 'frow', 'fcol'), may hold values from -0.5 to 5, as said below
- own_part: float32 [32, 2, 512, 512], P('leaf', None, 'frow', 'fcol'), may hold values from -0.5 to 1.5, as said below
- child_maps: int32 [48, 4, 7], replicated, may hold values from 0 to 7, as said below
Outputs:
- factor_panel: float32 [32, 4096, 512], P('leaf', 'frow', 'fcol')
Inputs may be any that keep to these rules, and one draw needn't show every extreme that they name: child_maps[c, q] lists 7 distinct parent block numbers of quarter q in increasing order. Each child_update[i] is symmetric positive definite. Each own_part[i, l] is symmetric positive definite.
All inputs are finite; a program needn't handle non-finite values.
Results may differ from a plain program's by a relative error of at most 0.0003.
Values sent between devices are 32-bit elements; how exact they have to be, the bound alone decides.
A program may use at most 128 MiB of HBM per device.

v0:
```python
import jax
import jax.numpy as jnp
from jax import lax
from jax.sharding import PartitionSpec as P

BLOCK = 128


def from_partner(x, axis, distance):
    return lax.ppermute(x, axis, [(i, i ^ 1 << distance) for i in range(lax.axis_size(axis))])


def broadcast(x, axis, root):
    mine = lax.axis_index(axis) == root
    return lax.psum(jnp.where(mine, x, jnp.zeros_like(x)), axis)


def block_order(map_row, parent_blocks, child_blocks):
    parent_slots = jnp.arange(parent_blocks, dtype=jnp.int32)
    matches = map_row[None, :] == parent_slots[:, None]
    present = jnp.any(matches, axis=1)
    child_slot = jnp.argmax(matches.astype(jnp.int32), axis=1)
    return jnp.where(present, child_slot, jnp.int32(child_blocks))


def extend_tile(update_tile, row_map, col_map, parent_blocks, kept_blocks):
    child_blocks = update_tile.shape[0] // BLOCK
    blocks = update_tile.reshape(child_blocks, BLOCK, child_blocks, BLOCK)
    row_order = block_order(row_map, parent_blocks, child_blocks)
    col_order = block_order(col_map, parent_blocks, child_blocks)[:kept_blocks]
    placed = jnp.take(blocks, col_order, axis=2, mode="fill", fill_value=0.0)
    placed = jnp.take(placed, row_order, axis=0, mode="fill", fill_value=0.0)
    return placed.reshape(parent_blocks * BLOCK, kept_blocks * BLOCK)


def pair_front(
    update_tile,
    own_blocks,
    own_maps,
    peer_maps,
    row_quarter,
    col_quarter,
    parent_blocks,
    bit_number,
):
    got_update, got_owns = from_partner((update_tile, own_blocks), "leaf", bit_number)
    front_tile = extend_tile(
        update_tile, own_maps[row_quarter], own_maps[col_quarter], parent_blocks, parent_blocks
    )
    front_tile = front_tile + extend_tile(
        got_update, peer_maps[row_quarter], peer_maps[col_quarter], parent_blocks, parent_blocks
    )
    return (front_tile, own_blocks + got_owns)


def on_device(child_update, own_part, child_maps):
    update_tile = child_update[0]
    own_blocks = own_part[0]
    pivots_local = own_part.shape[2]
    rows_local = update_tile.shape[0] + pivots_local
    parent_blocks = rows_local // BLOCK
    pivot_blocks = pivots_local // BLOCK
    level_count = own_part.shape[1]
    row_quarter = lax.axis_index("frow")
    col_quarter = lax.axis_index("fcol")
    leaf_index = lax.axis_index("leaf")
    leaf_count = lax.axis_size("leaf")
    map_offset = 0
    for merge_level in range(1, level_count + 1):
        bit_number = merge_level - 1
        own_child = map_offset + (leaf_index >> bit_number)
        peer_child = map_offset + (leaf_index >> bit_number ^ 1)
        own_maps = child_maps[own_child]
        peer_maps = child_maps[peer_child]
        is_top = merge_level == level_count
        front_tile = None
        if is_top:
            got_update, got_owns = from_partner((update_tile, own_blocks), "leaf", bit_number)
            column_part = extend_tile(
                update_tile,
                own_maps[row_quarter],
                own_maps[col_quarter],
                parent_blocks,
                pivot_blocks,
            )
            column_part = column_part + extend_tile(
                got_update,
                peer_maps[row_quarter],
                peer_maps[col_quarter],
                parent_blocks,
                pivot_blocks,
            )
            own_blocks = own_blocks + got_owns
        else:
            front_tile, own_blocks = pair_front(
                update_tile,
                own_blocks,
                own_maps,
                peer_maps,
                row_quarter,
                col_quarter,
                parent_blocks,
                bit_number,
            )
            column_part = front_tile[:, :pivots_local]
        column_part = column_part.at[:pivots_local, :].add(own_blocks[0])
        own_blocks = own_blocks[1:]
        gathered = lax.all_gather(column_part, "fcol", axis=1, tiled=True)
        pivot_matrix = lax.all_gather(gathered[:pivots_local], "frow", axis=0, tiled=True)
        pivot_factor = jnp.linalg.cholesky(pivot_matrix)
        factor_here = lax.linalg.triangular_solve(
            pivot_factor, gathered[pivots_local:], left_side=False, lower=True, transpose_a=True
        )
        if is_top:
            pivot_rows = lax.dynamic_slice_in_dim(
                pivot_factor, row_quarter * pivots_local, pivots_local, 0
            )
            panel_rows = jnp.concatenate([pivot_rows, factor_here], axis=0)
            out_piece = lax.dynamic_slice_in_dim(
                panel_rows, col_quarter * pivots_local, pivots_local, 1
            )
            return out_piece[None]
        factor_there = broadcast(factor_here, "frow", col_quarter)
        product = lax.dot_general(
            factor_here,
            factor_there,
            (((1,), (1,)), ((), ())),
            precision=lax.Precision.HIGHEST,
            preferred_element_type=jnp.float32,
        )
        update_tile = front_tile[pivots_local:, pivots_local:] - product
        map_offset = map_offset + (leaf_count >> bit_number)
    return update_tile[None]


def solution(mesh):
    in_specs = (P("leaf", "frow", "fcol"), P("leaf", None, "frow", "fcol"), P())
    out_specs = P("leaf", "frow", "fcol")
    return jax.shard_map(
        on_device, mesh=mesh, in_specs=in_specs, out_specs=out_specs, check_vma=False
    )
```

profile of v0, /device:TPU:1, one launch (start us, length us, event | category | flops | bytes accessed | tf_op | source)
XLA Modules:
  0.0 679.3 jit_solution(8117901682524504830)
XLA Ops:
  6.5 8.8 %collective-permute-start = (f32[896,896]{1,0:T(8,128)}, f32[896,896]{1,0:T(8,128)}, u32[]{:S(2)}, u32[]{:S(2)}) collective-permute-start(f32[896,896]{1,0:T(8,128)} %bitcast.160), channel_id=1, source_target_pairs={{0,16},{16,0},{32,48},{48,32},{64,80},{80,64},{96,112},{112,96},{1... | collective-permute-start | bytes 9633800 | tf_op jit(solution)/shard_map/ppermute | solution.py:10
  18.3 4.6 reshape_squeeze.3
  38.7 4.8 gather_fusion.1
  44.4 4.6 reshape.156
  60.8 4.8 gather_fusion.3
  73.8 37.6 %all-gather.5.cloned.1.call-done = f32[1024,512]{0,1:T(8,128)} async-done(((f32[1024,128]{0,1:T(8,128)}), f32[1024,512]{0,1:T(8,128)}) %all-gather.5.cloned.1.call-update) | async-done | bytes 2097168 | tf_op jit(solution)/shard_map/all_gather | solution.py:108
  113.3 32.9 %all-gather.7.cloned.1.call-done = f32[512,512]{0,1:T(8,128)} async-done(((f32[128,512]{0,1:T(8,128)}), f32[512,512]{0,1:T(8,128)}) %all-gather.7.cloned.1.call-update) | async-done | bytes 1048592 | tf_op jit(solution)/shard_map/all_gather | solution.py:109
  149.2 11.7 %cholesky.286 = f32[128,128]{1,0:T(8,128)S(1)} custom-call(f32[128,128]{1,0:T(8,128)S(1)} %cholesky.426), custom_call_target="Cholesky" | custom-call | tf_op jit(solution)/shard_map/jit(cholesky)/cholesky | solution.py:110
  161.1 9.8 %custom-call.27 = f32[1,128,128]{1,2,0:T(8,128)S(1)} custom-call(f32[1,128,128]{2,1,0:T(8,128)S(1)} %get-tuple-element.139), custom_call_target="InvertDiagBlocksLowerTriangular" | custom-call | tf_op jit(solution)/shard_map/jit(cholesky)/cholesky | solution.py:110
  171.6 11.7 %cholesky.305 = f32[128,128]{1,0:T(8,128)S(1)} custom-call(f32[128,128]{1,0:T(8,128)S(1)} %cholesky.430), custom_call_target="Cholesky" | custom-call | tf_op jit(solution)/shard_map/jit(cholesky)/cholesky | solution.py:110
  184.6 10.2 %custom-call.28 = f32[1,128,128]{1,2,0:T(8,128)S(1)} custom-call(f32[1,128,128]{2,1,0:T(8,128)S(1)} %get-tuple-element.136), custom_call_target="InvertDiagBlocksLowerTriangular" | custom-call | tf_op jit(solution)/shard_map/jit(cholesky)/cholesky | solution.py:110
  195.4 11.7 %cholesky.326 = f32[128,128]{1,0:T(8,128)S(1)} custom-call(f32[128,128]{1,0:T(8,128)S(1)} %cholesky.435), custom_call_target="Cholesky" | custom-call | tf_op jit(solution)/shard_map/jit(cholesky)/cholesky | solution.py:110
  207.9 9.8 %custom-call.29 = f32[1,128,128]{1,2,0:T(8,128)S(1)} custom-call(f32[1,128,128]{2,1,0:T(8,128)S(1)} %get-tuple-element.133), custom_call_target="InvertDiagBlocksLowerTriangular" | custom-call | tf_op jit(solution)/shard_map/jit(cholesky)/cholesky | solution.py:110
  218.3 11.7 %cholesky.343 = f32[128,128]{1,0:T(8,128)S(1)} custom-call(f32[128,128]{1,0:T(8,128)S(1)} %convolution_subtract_fusion.10), custom_call_target="Cholesky" | custom-call | tf_op jit(solution)/shard_map/jit(cholesky)/cholesky | solution.py:110
  233.6 7.7 %while.7 = (s32[]{:T(128)}, f32[512,512]{1,0:T(8,128)S(1)}, s32[4,2]{0,1:T(2,128)S(1)}, f32[4,128,128]{2,1,0:T(8,128)S(1)}, s32[]{:T(128)}) while((s32[]{:T(128)}, f32[512,512]{1,0:T(8,128)S(1)}, s32[4,2]{0,1:T(2,128)S(1)}, f32[4,128,128]{2,1,0:T(8,128)S(1)}, s32[]{:T(128)}) %tuple.96), condition=%wide.while_cond.2, body=%wide.while_body.2.sunk | while | flops 2 | bytes 131181 | solution.py:111
  241.3 39.3 %custom-call.30 = f32[4,128,128]{1,2,0:T(8,128)S(1)} custom-call(f32[4,128,128]{2,1,0:T(8,128)S(1)} %get-tuple-element.76), custom_call_target="InvertDiagBlocksLowerTriangular" | custom-call | tf_op jit(solution)/shard_map/triangular_solve/custom-call.3 | solution.py:111
  294.7 4.3 copy.65
  299.0 63.7 %all-reduce.3.cloned.1.call-done = f32[896,512]{0,1:T(8,128)} async-done(((f32[896,512]{0,1:T(8,128)}), f32[896,512]{0,1:T(8,128)}) %all-reduce.3.cloned.1.call-update) | async-done | bytes 1835024 | tf_op jit(solution)/shard_map/psum | solution.py:15
  362.7 9.5 %convolution_subtract_fusion = f32[896,896]{0,1:T(8,128)} fusion(f32[896,896]{0,1:T(8,128)} %copy.65, f32[896,512]{0,1:T(8,128)} %all-reduce.3.cloned.1.call-done, f32[896,128]{0,1:T(8,128)S(1)} %fusion.61, f32[896,128]{0,1:T(8,128)S(1)} %fusion.62, f32[896,128]{0,1:T(8,128)S(1)} %fusion.63, f32[896,128]{0,1:T(8,128)S(1)} %bitcast.153), kind=kOutput, calls=%fused_computation.19 | convolution fusion | flops 4934680576 | bytes 10092544 | tf_op jit(solution)/shard_map/dot_general | solution.py:124
  380.7 4.6 reshape.330
  395.5 49.2 %collective-permute-done.2 = f32[896,896]{0,1:T(8,128)S(1)} collective-permute-done((f32[896,896]{0,1:T(8,128)}, f32[896,896]{0,1:T(8,128)S(1)}, u32[]{:S(2)}, u32[]{:S(2)}) %collective-permute-start.2) | collective-permute-done | bytes 3211296 | tf_op jit(solution)/shard_map/ppermute | solution.py:10
  450.8 39.7 %all-gather.9.cloned.1.call-done = f32[1024,512]{0,1:T(8,128)} async-done(((f32[1024,128]{0,1:T(8,128)}), f32[1024,512]{0,1:T(8,128)}) %all-gather.9.cloned.1.call-update) | async-done | bytes 2097168 | tf_op jit(solution)/shard_map/all_gather | solution.py:108
  492.2 33.0 %all-gather.11.cloned.1.call-done = f32[512,512]{0,1:T(8,128)} async-done(((f32[128,512]{0,1:T(8,128)}), f32[512,512]{0,1:T(8,128)}) %all-gather.11.cloned.1.call-update) | async-done | bytes 1048592 | tf_op jit(solution)/shard_map/all_gather | solution.py:109
  528.2 11.7 %cholesky.358 = f32[128,128]{1,0:T(8,128)S(1)} custom-call(f32[128,128]{1,0:T(8,128)S(1)} %cholesky.439), custom_call_target="Cholesky" | custom-call | tf_op jit(solution)/shard_map/jit(cholesky)/cholesky | solution.py:110
  540.1 9.8 %custom-call.31 = f32[1,128,128]{1,2,0:T(8,128)S(1)} custom-call(f32[1,128,128]{2,1,0:T(8,128)S(1)} %get-tuple-element.129), custom_call_target="InvertDiagBlocksLowerTriangular" | custom-call | tf_op jit(solution)/shard_map/jit(cholesky)/cholesky | solution.py:110
  550.6 11.7 %cholesky.377 = f32[128,128]{1,0:T(8,128)S(1)} custom-call(f32[128,128]{1,0:T(8,128)S(1)} %cholesky.443), custom_call_target="Cholesky" | custom-call | tf_op jit(solution)/shard_map/jit(cholesky)/cholesky | solution.py:110
  563.6 10.0 %custom-call.32 = f32[1,128,128]{1,2,0:T(8,128)S(1)} custom-call(f32[1,128,128]{2,1,0:T(8,128)S(1)} %get-tuple-element.126), custom_call_target="InvertDiagBlocksLowerTriangular" | custom-call | tf_op jit(solution)/shard_map/jit(cholesky)/cholesky | solution.py:110
  574.2 11.7 %cholesky.398 = f32[128,128]{1,0:T(8,128)S(1)} custom-call(f32[128,128]{1,0:T(8,128)S(1)} %cholesky.448), custom_call_target="Cholesky" | custom-call | tf_op jit(solution)/shard_map/jit(cholesky)/cholesky | solution.py:110
  586.6 9.8 %custom-call.33 = f32[1,128,128]{1,2,0:T(8,128)S(1)} custom-call(f32[1,128,128]{2,1,0:T(8,128)S(1)} %get-tuple-element.123), custom_call_target="InvertDiagBlocksLowerTriangular" | custom-call | tf_op jit(solution)/shard_map/jit(cholesky)/cholesky | solution.py:110
  597.1 11.7 %cholesky.415 = f32[128,128]{1,0:T(8,128)S(1)} custom-call(f32[128,128]{1,0:T(8,128)S(1)} %convolution_subtract_fusion.9), custom_call_target="Cholesky" | custom-call | tf_op jit(solution)/shard_map/jit(cholesky)/cholesky | solution.py:110
  612.4 7.9 %while.8 = (s32[]{:T(128)}, f32[512,512]{1,0:T(8,128)S(1)}, s32[4,2]{0,1:T(2,128)S(1)}, f32[4,128,128]{2,1,0:T(8,128)S(1)}, s32[]{:T(128)}) while((s32[]{:T(128)}, f32[512,512]{1,0:T(8,128)S(1)}, s32[4,2]{0,1:T(2,128)S(1)}, f32[4,128,128]{2,1,0:T(8,128)S(1)}, s32[]{:T(128)}) %tuple.112), condition=%wide.while_cond.2.clone, body=%wide.while_body.2.clone.sunk | while | flops 2 | bytes 131181 | solution.py:111
  620.4 39.3 %custom-call.34 = f32[4,128,128]{1,2,0:T(8,128)S(1)} custom-call(f32[4,128,128]{2,1,0:T(8,128)S(1)} %get-tuple-element.77), custom_call_target="InvertDiagBlocksLowerTriangular" | custom-call | tf_op jit(solution)/shard_map/triangular_solve/custom-call.3 | solution.py:111
  (180 shorter events, 125.9 us)
Async XLA Ops:
  6.5 104.8 %all-gather.5.cloned.1.call-start = ((), (), s32[]{:S(2)}) async-start(), calls=%async_computation | async-start | bytes 2621440 | tf_op jit(solution)/shard_map/all_gather | solution.py:108
  6.5 37.9 %collective-permute-start = (f32[896,896]{1,0:T(8,128)}, f32[896,896]{1,0:T(8,128)}, u32[]{:S(2)}, u32[]{:S(2)}) collective-permute-start(f32[896,896]{1,0:T(8,128)} %bitcast.160), channel_id=1, source_target_pairs={{0,16},{16,0},{32,48},{48,32},{64,80},{80,64},{96,112},{112,96},{1... | collective-permute-start | bytes 9633800 | tf_op jit(solution)/shard_map/ppermute | solution.py:10
  16.3 27.2 %collective-permute-start.1 = (f32[2,128,128]{1,2,0:T(8,128)S(1)}, f32[2,128,128]{1,2,0:T(8,128)}, u32[]{:S(2)}, u32[]{:S(2)}) collective-permute-start(f32[2,128,128]{1,2,0:T(8,128)S(1)} %bitcast.162), channel_id=1, source_target_pairs={{0,16},{16,0},{32,48},{48,32},{64,80},{80,64},{96,112},{112,96},{1... | collective-permute-start | bytes 393224 | tf_op jit(solution)/shard_map/ppermute | solution.py:10
  22.9 2.6 copy-start.5
  70.6 1.9 copy-start
  72.9 0.8 copy-start.2
  73.7 72.5 %all-gather.7.cloned.1.call-start = ((), (), s32[]{:S(2)}) async-start(), calls=%async_computation.1 | async-start | bytes 1310720 | tf_op jit(solution)/shard_map/all_gather | solution.py:109
  113.0 249.7 %all-reduce.3.cloned.1.call-start = ((), (), s32[]{:S(2)}) async-start(), calls=%async_computation.2 | async-start | bytes 3670016 | tf_op jit(solution)/shard_map/psum | solution.py:15
  290.8 199.6 %all-gather.9.cloned.1.call-start = ((), (), s32[]{:S(2)}) async-start(), calls=%async_computation.3 | async-start | bytes 2621440 | tf_op jit(solution)/shard_map/all_gather | solution.py:108
  372.2 72.5 %collective-permute-start.2 = (f32[896,896]{0,1:T(8,128)}, f32[896,896]{0,1:T(8,128)S(1)}, u32[]{:S(2)}, u32[]{:S(2)}) collective-permute-start(f32[896,896]{0,1:T(8,128)} %convolution_subtract_fusion), channel_id=1, source_target_pairs={{0,32},{16,48},{32,0},{48,16},{64,96},{80,112},{96,64},{112,80},{1... | collective-permute-start | bytes 9633800 | tf_op jit(solution)/shard_map/ppermute | solution.py:10
  378.6 70.9 %collective-permute-start.3 = (f32[1,128,128]{1,2,0:T(8,128)S(1)}, f32[1,128,128]{1,2,0:T(8,128)S(1)}, u32[]{:S(2)}, u32[]{:S(2)}) collective-permute-start(f32[1,128,128]{1,2,0:T(8,128)S(1)} %slice.267), channel_id=1, source_target_pairs={{0,32},{16,48},{32,0},{48,16},{64,96},{80,112},{96,64},{112,80},{1... | collective-permute-start | bytes 196616 | tf_op jit(solution)/shard_map/ppermute | solution.py:10
  446.7 2.2 copy-start.3
  449.5 0.8 copy-start.1
  450.3 74.8 %all-gather.11.cloned.1.call-start = ((), (), s32[]{:S(2)}) async-start(), calls=%async_computation.4 | async-start | bytes 1310720 | tf_op jit(solution)/shard_map/all_gather | solution.py:109
  659.7 1.7 copy-start.4
Sparse Core Ops, SparseCore 0:
  73.8 37.4 all-gather.4
  113.4 32.7 all-gather.6
  291.0 71.7 all-reduce.2
  450.5 39.9 all-gather.8
  492.4 32.7 all-gather.10
where the time goes:
time: 689 us; the launch traced here: 679 us
  other arithmetic  260 us (38%)
  waiting for transfers between devices  256 us (37%)
  local copies, waits for them, and re-layouts  93.1 us (14%)
  matrix products  33.3 us (5%)
  between operations  19.4 us (3%)
  starting transfers between devices  16.7 us (2%)
    another operation x30, other arithmetic, on_device(): pivot_factor = jnp.linalg.cholesky(pivot_matrix)  159 us
    another operation x5, other arithmetic, on_device(): lax.linalg.triangular_solve(pivot_factor, gathered[pivots_local:], left_s...  79.4 us
    all_gather x2, waiting for transfers between devices, on_device(): gathered = lax.all_gather(column_part, 'fcol', axis=1, tiled=True)  77.3 us
    all_gather x2, waiting for transfers between devices, on_device(): lax.all_gather(gathered[:pivots_local], 'frow', axis=0, tiled=True)  65.9 us
    psum x1, waiting for transfers between devices, broadcast(): return lax.psum(jnp.where(mine, x, jnp.zeros_like(x)), axis)  63.7 us
    ppermute x4, waiting for transfers between devices, from_partner(): lax.ppermute(x, axis, [(i, i ^ 1 << distance) for i in range(lax.axis_siz...  49.2 us
    another operation x14, matrix products, on_device(): lax.linalg.triangular_solve(pivot_factor, gathered[pivots_local:], left_s...  20.1 us
    ppermute x4, starting transfers between devices, from_partner(): lax.ppermute(x, axis, [(i, i ^ 1 << distance) for i in range(lax.axis_siz...  16 us
  transfers between devices with their start and end apart: 9, of which 6 were waited for; matrix products, arithmetic and copies ran while one was open for 8% of the time, Pallas kernels for 0%

commit v1 on v0

v1 whole, which is shorter than its diff:
```python
import jax
import jax.numpy as jnp
from jax import lax
from jax.experimental import pallas as pl
from jax.experimental.pallas import tpu as pltpu
from jax.sharding import PartitionSpec as P

HI = lax.Precision.HIGHEST
MESH = pl.DeviceIdType.MESH


def mm(a, b, ca, cb):
    return lax.dot_general(a, b, (((ca,), (cb,)), ((), ())), precision=HI, preferred_element_type=jnp.float32)

def bc(x):
    return jnp.broadcast_to(x, (8, 128))

def small_factor(cols):
    a = {}
    for j in range(8):
        for i in range(j, 8):
            a[i, j] = bc(cols[j][i:i + 1, :])
    low, inv, x = {}, {}, {}
    for j in range(8):
        inv[j] = lax.rsqrt(a[j, j])
        for i in range(j + 1, 8):
            low[i, j] = a[i, j] * inv[j]
        for k in range(j + 1, 8):
            for i in range(k, 8):
                a[i, k] = a[i, k] - low[i, j] * low[k, j]
    for j in range(8):
        x[j, j] = inv[j]
        for i in range(j + 1, 8):
            t = low[i, j] * x[j, j]
            for k in range(j + 1, i):
                t = t + low[i, k] * x[k, j]
            x[i, j] = -(inv[i] * t)
    return x

def tree(terms):
    while len(terms) > 1:
        terms = [terms[i] + terms[i + 1] if i + 1 < len(terms) else terms[i] for i in range(0, len(terms), 2)]
    return terms[0]

def diag_factor(read, write_x, write_u):
    lane = lax.broadcasted_iota(jnp.int32, (8, 128), 1)
    sub = lax.broadcasted_iota(jnp.int32, (8, 128), 0)
    rows = [read(i) for i in range(16)]
    for s in range(16):
        base = 8 * s
        top = rows[s]
        here = (lane >= base) & (lane < base + 8)
        cols = [bc(top[:, base + j:base + j + 1]) for j in range(8)]
        x = small_factor(cols)
        p = []
        for j in range(8):
            v = x[7, j]
            for i in range(6, j - 1, -1):
                v = jnp.where(sub <= i, x[i, j], v)
            p.append(jnp.where(sub >= j, v, 0.0) if j else v)
        q = []
        for j in range(8):
            v = x[j, j]
            for i in range(j - 1, -1, -1):
                v = jnp.where(sub <= i, x[j, i], v)
            q.append(jnp.where(sub <= j, v, 0.0) if j < 7 else v)
        unit = jnp.where(here, (lane - base == sub).astype(jnp.float32), top)
        w = tree([p[j] * bc(unit[j:j + 1, :]) for j in range(8)])
        write_x(s, jnp.where(lane < base + 8, w, 0.0))
        if write_u is not None:
            u = tree([p[j] * bc(top[j:j + 1, :]) for j in range(8)])
            write_u(s, jnp.where(lane - base >= sub, u, 0.0))
        if s == 15:
            break
        g = tree([q[j] * bc(w[j:j + 1, :]) for j in range(8)])
        gr = [bc(g[j:j + 1, :]) for j in range(8)]
        for i in range(s + 1, 16):
            m = [bc(rows[i][:, base + j:base + j + 1]) for j in range(8)]
            rows[i] = jnp.where(here, 0.0, rows[i]) - tree([m[j] * gr[j] for j in range(8)])

def block_factor(s_ref, x_ref, u_ref, width, z_ref=None):
    def step(j, _):
        cj = pl.multiple_of(j * 128, 128)
        def wx(s, v):
            x_ref[8 * s:8 * s + 8, :] = v
        def wu(s, v):
            u_ref[j, 8 * s:8 * s + 8, :] = v
        diag_factor(lambda i: s_ref[j, 8 * i:8 * i + 8, pl.ds(cj, 128)], wx, wu if u_ref is not None else None)
        r_i = lax.broadcasted_iota(jnp.int32, (128, 128), 0)
        c_i = lax.broadcasted_iota(jnp.int32, (128, 128), 1)
        s_ref[j, :, pl.ds(cj, 128)] = (r_i == c_i).astype(jnp.float32)
        s_ref[j] = mm(x_ref[...], s_ref[j], 1, 0)
        def trail(i, _):
            ci = pl.multiple_of(i * 128, 128)
            s_ref[i, :, pl.ds(cj, 128)] = jnp.zeros((128, 128), jnp.float32)
            s_ref[i] = s_ref[i] - mm(s_ref[j, :, pl.ds(ci, 128)], s_ref[j], 0, 0)
            return 0
        lax.fori_loop(j + 1, 4, trail, 0)
        if z_ref is not None:
            lanes = lax.broadcasted_iota(jnp.int32, (128, 512), 1)
            li = jnp.where(lanes < (j + 1) * 128, s_ref[j, :, :512], 0.0)
            z_ref[...] += mm(li, s_ref[j, :, 512:640], 0, 0)
        return 0
    if z_ref is not None:
        z_ref[...] = jnp.zeros_like(z_ref)
    lax.fori_loop(0, 4, step, 0)


def pick(condition):
    return jnp.where(condition, jnp.float32(1.0), jnp.float32(0.0))


def row_coefficients(maps, child, quarter):
    entries = [maps[child, quarter, t] for t in range(7)]
    same = [pick(entries[p] == p) if p < 7 else None for p in range(8)]
    above = [pick(entries[p - 1] == p) if p > 0 else None for p in range(8)]
    return same, above


def place(same, above, p, blocks):
    if p == 0:
        return blocks(0) * same[0]
    if p == 7:
        return blocks(6) * above[7]
    return blocks(p) * same[p] + blocks(p - 1) * above[p]


def kernel(
    update, own, maps, out,
    mine, theirs, own_mine, own_theirs, tile1, s1, a1, v_mine, v_theirs, z, x, u, head_mine, head_theirs, tile2, s2, a2,
    local, ex_s, ex_r, f1_s, f1_r, b1_s, b1_r, a1_s, a1_r, zx_s, zx_r, f2_s, f2_r, a2_s, a2_r,
):
    leaf, r, c = lax.axis_index("leaf"), lax.axis_index("frow"), lax.axis_index("fcol")
    twin = leaf + 1 - 2 * lax.rem(leaf, 2)
    pair = leaf // 2
    other = pair + 1 - 2 * lax.rem(pair, 2)
    far = other * 2 + lax.rem(leaf, 2)
    rc, cc = pl.multiple_of(r * 128, 128), pl.multiple_of(c * 128, 128)

    loads = [
        pltpu.make_async_copy(update.at[pl.ds(0, 128), pl.ds(0, 256)], mine.at[pl.ds(0, 128)], local.at[0]),
        pltpu.make_async_copy(own, own_mine, local.at[1]),
        pltpu.make_async_copy(update.at[pl.ds(128, 768), pl.ds(0, 256)], mine.at[pl.ds(128, 768)], local.at[2]),
    ]
    for copy in loads:
        copy.start()

    def send(src, dst, s, t, to):
        copy = pltpu.make_async_remote_copy(
            src_ref=src, dst_ref=dst, send_sem=s, recv_sem=t, device_id=to, device_id_type=MESH
        )
        return copy

    plane = [(i, j) for i in range(4) for j in range(4) if (i, j) != (0, 0)]

    def at(i, j):
        return {"frow": lax.rem(r + i, 4), "fcol": lax.rem(c + j, 4)}

    barrier = pltpu.get_barrier_semaphore()
    pl.semaphore_signal(barrier, inc=1, device_id={"leaf": twin}, device_id_type=MESH)
    pl.semaphore_signal(barrier, inc=1, device_id={"leaf": far}, device_id_type=MESH)
    for i, j in plane:
        pl.semaphore_signal(barrier, inc=1, device_id=at(i, j), device_id_type=MESH)
    pl.semaphore_wait(barrier, 17)

    swaps = [
        send(update.at[pl.ds(0, 128), pl.ds(0, 256)], theirs.at[pl.ds(0, 128)], ex_s.at[0], ex_r.at[0], {"leaf": twin}),
        send(own, own_theirs, ex_s.at[1], ex_r.at[1], {"leaf": twin}),
        send(update.at[pl.ds(128, 768), pl.ds(0, 256)], theirs.at[pl.ds(128, 768)], ex_s.at[2], ex_r.at[2], {"leaf": twin}),
    ]
    for copy in swaps:
        copy.start()

    sides = []
    for ref, child in ((mine, leaf), (theirs, twin)):
        same, above = row_coefficients(maps, child, r)
        first, second = maps[child, c, 0], maps[child, c, 1]
        sides.append((ref, same, above, pick(first == 0), pick(first == 1), pick(second == 1)))

    def front1(p, column):
        total = None
        for ref, same, above, zero, one, two in sides:
            def blocks(t):
                left = ref[128 * t:128 * t + 128, 0:128]
                if column == 0:
                    return left * zero
                return left * one + ref[128 * t:128 * t + 128, 128:256] * two
            part = place(same, above, p, blocks)
            total = part if total is None else total + part
        return total

    loads[0].wait()
    loads[1].wait()
    swaps[0].wait_recv()
    swaps[1].wait_recv()
    pivot = front1(0, 0) + (own_mine[0] + own_theirs[0])
    side = front1(0, 1)
    tile1[0] = pivot
    tile1[1] = side
    s1[r, :, pl.ds(cc, 128)] = pivot
    s1[r, :, 512:640] = side

    def spread(tile, store, s, t):
        return [send(tile, store.at[r, :, pl.ds(cc, 128)], s.at[4 * i + j], t.at[4 * i + j], at(i, j)) for i, j in plane]

    def gather(tile, store, s, t):
        copies = []
        for i, j in plane:
            fr, fc = lax.rem(r + 4 - i, 4), lax.rem(c + 4 - j, 4)
            place_ = store.at[fr, :, pl.ds(pl.multiple_of(fc * 128, 128), 128)]
            copies.append(send(tile, place_, s.at[4 * i + j], t.at[4 * i + j], at(i, j)))
        return copies

    def rows_out(a, s, t):
        block = a.at[:, pl.ds(cc, 128)]
        return [send(block, block, s.at[j], t.at[j], at(0, j)) for j in range(1, 4)]

    def rows_in(a, s, t):
        copies = []
        for j in range(1, 4):
            fc = pl.multiple_of(lax.rem(c + 4 - j, 4) * 128, 128)
            block = a.at[:, pl.ds(fc, 128)]
            copies.append(send(block, block, s.at[j], t.at[j], at(0, j)))
        return copies

    out1 = spread(tile1.at[0], s1, f1_s, f1_r)
    side1 = [send(tile1.at[1], s1.at[r, :, pl.ds(512, 128)], b1_s.at[i], b1_r.at[i], at(i, 0)) for i in range(1, 4)]
    for copy in out1 + side1:
        copy.start()

    loads[2].wait()
    swaps[2].wait_recv()
    for p in range(1, 8):
        a1[128 * (p - 1):128 * p, pl.ds(cc, 128)] = front1(p, 0)
    rows1 = rows_out(a1, a1_s, a1_r)
    for copy in rows1:
        copy.start()
    for p in range(1, 8):
        v_mine[128 * (p - 1):128 * p, :] = front1(p, 1)

    for copy in gather(tile1.at[0], s1, f1_s, f1_r):
        copy.wait_recv()
    for i in range(1, 4):
        send(
            tile1.at[1], s1.at[lax.rem(r + 4 - i, 4), :, pl.ds(512, 128)], b1_s.at[i], b1_r.at[i], at(i, 0)
        ).wait_recv()
    block_factor(s1, x, None, 640, z)
    for copy in rows_in(a1, a1_s, a1_r):
        copy.wait_recv()

    sides2 = []
    for child, ref in ((32 + pair, v_mine), (32 + other, v_theirs)):
        same, above = row_coefficients(maps, child, r)
        sides2.append((ref, same, above, pick(maps[child, c, 0] == 0)))

    v_mine[0:128, :] = v_mine[0:128, :] - mm(a1[0:128, :], z[...], 1, 0)
    _, same, _, zero = sides2[0]
    head_mine[...] = v_mine[0:128, :] * same[0] * zero + (own_mine[1] + own_theirs[1])
    head = send(head_mine, head_theirs, zx_s.at[0], zx_r.at[0], {"leaf": far})
    head.start()
    for lo in range(128, 896, 256):
        v_mine[lo:lo + 256, :] = v_mine[lo:lo + 256, :] - mm(a1[lo:lo + 256, :], z[...], 1, 0)
    rest = send(v_mine, v_theirs, zx_s.at[1], zx_r.at[1], {"leaf": far})
    rest.start()

    head.wait_recv()
    pivot = head_mine[...] + head_theirs[...]
    tile2[...] = pivot
    s2[r, :, pl.ds(cc, 128)] = pivot
    out2 = spread(tile2, s2, f2_s, f2_r)
    for copy in out2:
        copy.start()
    rest.wait_recv()
    for p in range(1, 8):
        total = None
        for ref, same, above, zero in sides2:
            part = place(same, above, p, lambda t: ref[128 * t:128 * t + 128, :]) * zero
            total = part if total is None else total + part
        a2[128 * (p - 1):128 * p, pl.ds(cc, 128)] = total
    rows2 = rows_out(a2, a2_s, a2_r)
    for copy in rows2:
        copy.start()
    for copy in gather(tile2, s2, f2_s, f2_r):
        copy.wait_recv()
    block_factor(s2, x, u, 512)
    for copy in rows_in(a2, a2_s, a2_r):
        copy.wait_recv()

    below = s2[c, :, pl.ds(rc, 128)] * pick(r > c) + u[c] * pick(r == c)
    out[0:128, :] = below.T
    lanes = lax.broadcasted_iota(jnp.int32, (128, 512), 1)
    inverse = jnp.where(lanes < (c + 1) * 128, s2[c], 0.0)
    for lo in range(0, 896, 128):
        out[128 + lo:256 + lo, :] = mm(a2[lo:lo + 128, :], inverse, 1, 1)
    for copy in swaps + out1 + side1 + rows1 + [head, rest] + out2 + rows2:
        copy.wait_send()


def on_device(child_update, own_part, child_maps):
    shapes = [
        (896, 256), (896, 256), (2, 128, 128), (2, 128, 128), (2, 128, 128), (4, 128, 640), (896, 512), (896, 128), (896, 128),
        (512, 128), (128, 128), (4, 128, 128), (128, 128), (128, 128), (128, 128), (4, 128, 512), (896, 512),
    ]
    sems = [3, 3, 3, 16, 16, 4, 4, 4, 4, 2, 2, 16, 16, 4, 4]
    panel = pl.pallas_call(
        kernel,
        out_shape=jax.ShapeDtypeStruct((1024, 128), jnp.float32),
        in_specs=[
            pl.BlockSpec(memory_space=pl.ANY),
            pl.BlockSpec(memory_space=pl.ANY),
            pl.BlockSpec(memory_space=pltpu.SMEM),
        ],
        out_specs=pl.BlockSpec(memory_space=pltpu.VMEM),
        scratch_shapes=[pltpu.VMEM(s, jnp.float32) for s in shapes] + [pltpu.SemaphoreType.DMA((n,)) for n in sems],
        compiler_params=pltpu.CompilerParams(collective_id=0, has_side_effects=True, vmem_limit_bytes=48 << 20),
        name="merge",
    )(child_update[0], own_part[0], child_maps)
    return panel[None]


def solution(mesh):
    in_specs = (P("leaf", "frow", "fcol"), P("leaf", None, "frow", "fcol"), P())
    out_specs = P("leaf", "frow", "fcol")
    return jax.shard_map(on_device, mesh=mesh, in_specs=in_specs, out_specs=out_specs, check_vma=False)
```

time: 689 us -> 108 us (0.16); the launches traced: 679 us -> 107 us
  other arithmetic: 260 us -> 0 us
  waiting for transfers between devices: 256 us -> 0 us
  Pallas kernels: 0 us -> 103 us
  local copies, waits for them, and re-layouts: 93.1 us -> 4.43 us
  matrix products: 33.3 us -> 0 us
  between operations: 19.4 us -> 0.02 us
  starting transfers between devices: 16.7 us -> 0 us
    another operation x45 -> x0, other arithmetic: 245 us -> none  [the longest x30 159 us: on_device(): pivot_factor = jnp.linalg.cholesky(pivot_matrix)]
    all_gather x4 -> x0, waiting for transfers between devices: 143 us -> none  [the longest x2 77.3 us: on_device(): gathered = lax.all_gather(column_part, 'fcol', axis=1, tiled=True)]
    pallas_call x0 -> x1, Pallas kernels: none -> 103 us  [on_device(): pl.pallas_call(kernel, out_shape=jax.ShapeDtypeStruct((1024, 128), jnp.fl...]
    psum x1 -> x0, waiting for transfers between devices: 63.7 us -> none  [broadcast(): return lax.psum(jnp.where(mine, x, jnp.zeros_like(x)), axis)]
    ppermute x4 -> x0, waiting for transfers between devices: 49.2 us -> none  [from_partner(): lax.ppermute(x, axis, [(i, i ^ 1 << distance) for i in range(lax.axis_siz...]
    another operation x40 -> x0, local copies, waits for them, and re-layouts: 26 us -> none  [the longest x27 15.5 us: on_device(): lax.linalg.triangular_solve(pivot_factor, gathered[pivots_local:], left_s...]
    another operation x26 -> x0, matrix products: 23.8 us -> none  [the longest x14 20.1 us: on_device(): lax.linalg.triangular_solve(pivot_factor, gathered[pivots_local:], left_s...]
    gather x8 -> x0, local copies, waits for them, and re-layouts: 20 us -> none  [the longest x6 14.8 us: extend_tile(): placed = jnp.take(placed, row_order, axis=0, mode='fill', fill_value=0.0)]
  transfers between devices with their start and end apart: 9 -> 0, of which waited for: 6 -> 0; matrix products, arithmetic and copies ran while one was open for 8% -> 0% of each run, Pallas kernels for 0% -> 0%
where the time goes in v1:
time: 108 us; the launch traced here: 107 us
  Pallas kernels  103 us (95%)
  local copies, waits for them, and re-layouts  4.43 us (4%)
    pallas_call x1, Pallas kernels, on_device(): pl.pallas_call(kernel, out_shape=jax.ShapeDtypeStruct((1024, 128), jnp.fl...  103 us
    unnamed x6, local copies, waits for them, and re-layouts  4.43 us

profile of v1, /device:TPU:1, one launch (start us, length us, event | category | flops | bytes accessed | tf_op | source)
XLA Modules:
  0.0 107.0 jit_solution(13277845462154253037)
XLA Ops:
  0.0 0.8 copy.4.maps
  0.8 0.0 copy-start
  0.8 1.9 %copy-done = f32[1,896,896]{2,1,0:T(8,128)S(1)} copy-done((f32[1,896,896]{2,1,0:T(8,128)S(1)}, f32[1,896,896]{2,1,0:T(8,128)}, u32[]{:S(2)}) %copy-start) | copy-done | bytes 3211288
  2.7 0.0 copy-start.1
  2.7 0.9 copy-done.1
  3.6 102.6 %merge.1 = f32[1024,128]{1,0:T(8,128)S(1)} custom-call(f32[896,896]{1,0:T(8,128)S(1)} %bitcast.3, f32[2,128,128]{2,1,0:T(8,128)S(1)} %bitcast.5, s32[48,4,7]{2,1,0:T(4,128)S(1)} %copy.4.maps), custom_call_target="tpu_custom_call" | custom-call | tf_op jit(solution)/shard_map/merge/pallas_call | solution.py:305
  106.2 0.8 copy.6
Async XLA Ops:
  0.8 1.9 %copy-start = (f32[1,896,896]{2,1,0:T(8,128)S(1)}, f32[1,896,896]{2,1,0:T(8,128)}, u32[]{:S(2)}) copy-start(f32[1,896,896]{2,1,0:T(8,128)} %param.3) | copy-start | bytes 9633796
  2.7 0.9 copy-start.1

commit v2 on v1

v2 whole, which is shorter than its diff:
```python
import jax
import jax.numpy as jnp
from jax import lax
from jax.experimental import pallas as pl
from jax.experimental.pallas import tpu as pltpu
from jax.sharding import PartitionSpec as P

HI = lax.Precision.HIGHEST
MESH = pl.DeviceIdType.MESH
HALF = 64


def mm(a, b, ca, cb):
    return lax.dot_general(a, b, (((ca,), (cb,)), ((), ())), precision=HI, preferred_element_type=jnp.float32)


def spread_column(v, j):
    return jnp.broadcast_to(v[:, j:j + 1], (8, 128))


def spread_row(v, j):
    return jnp.broadcast_to(v[j:j + 1, :], (8, 128))


def tree(terms):
    while len(terms) > 1:
        terms = [terms[i] + terms[i + 1] if i + 1 < len(terms) else terms[i] for i in range(0, len(terms), 2)]
    return terms[0]


def diag_factor(rows, zero, x_ref, middle):
    lane = lax.broadcasted_iota(jnp.int32, (8, 128), 1)
    sub = lax.broadcasted_iota(jnp.int32, (8, 128), 0)
    c = [spread_column(rows[0], j) + zero for j in range(8)]
    for s in range(16):
        if s == 8:
            middle()
        base = 8 * s
        here = (lane >= base) & (lane < base + 8)
        more = s < 15
        a = {(i, j): spread_row(c[j], i) for j in range(8) for i in range(j, 8)}
        unit = jnp.where(here, (lane - base == sub).astype(jnp.float32), rows[s])
        w = [spread_row(unit, j) for j in range(8)]
        if more:
            y = [spread_column(rows[s + 1], base + j) for j in range(8)]
            d = [spread_column(rows[s + 1], base + 8 + j) for j in range(8)]
        low, inv = {}, {}
        for j in range(8):
            inv[j] = lax.rsqrt(a[j, j])
            for i in range(j + 1, 8):
                low[i, j] = a[i, j] * inv[j]
            for k in range(j + 1, 8):
                for i in range(k, 8):
                    a[i, k] = a[i, k] - low[i, j] * low[k, j]
            w[j] = w[j] * inv[j]
            for k in range(j + 1, 8):
                w[k] = w[k] - low[k, j] * w[j]
            if more:
                y[j] = y[j] * inv[j]
                for k in range(j + 1, 8):
                    y[k] = y[k] - low[k, j] * y[j]
                for k in range(8):
                    d[k] = d[k] - y[j] * spread_row(y[j], k)
        if more:
            c = d
            rows[s + 1] = jnp.where(here, 0.0, rows[s + 1]) - tree([y[j] * w[j] for j in range(8)])
            g = list(w)
            for j in range(7, -1, -1):
                g[j] = g[j] * inv[j]
                for k in range(j):
                    g[k] = g[k] - low[j, k] * g[j]
            for i in range(s + 2, 16):
                part = tree([spread_column(rows[i], base + j) * g[j] for j in range(8)])
                rows[i] = jnp.where(here, 0.0, rows[i]) - part
        done = w[7]
        for i in range(6, -1, -1):
            done = jnp.where(sub <= i, w[i], done)
        x_ref[base:base + 8, :] = jnp.where(lane < base + 8, done, 0.0)


def block_factor(s_ref, x_ref, u_ref, z_ref, zero_ref, before, middle, after):
    def step(j, _):
        cj = pl.multiple_of(j * 128, 128)
        before(j)
        zero = zero_ref[...]
        rows = [s_ref[j, 8 * i:8 * i + 8, pl.ds(cj, 128)] for i in range(16)]
        if u_ref is not None:
            u_ref[j] = s_ref[j, :, pl.ds(cj, 128)]
        diag_factor(rows, zero, x_ref, lambda: middle(j))
        after(j)
        r_i = lax.broadcasted_iota(jnp.int32, (128, 128), 0)
        c_i = lax.broadcasted_iota(jnp.int32, (128, 128), 1)
        s_ref[j, :, pl.ds(cj, 128)] = (r_i == c_i).astype(jnp.float32)
        s_ref[j] = mm(x_ref[...], s_ref[j], 1, 0)

        def trail(i, _):
            ci = pl.multiple_of(i * 128, 128)
            s_ref[i, :, pl.ds(cj, 128)] = jnp.zeros((128, 128), jnp.float32)
            s_ref[i] = s_ref[i] - mm(s_ref[j, :, pl.ds(ci, 128)], s_ref[j], 0, 0)
            return 0

        lax.fori_loop(j + 1, 4, trail, 0)
        if z_ref is not None:
            lanes = lax.broadcasted_iota(jnp.int32, (128, 512), 1)
            inverse = jnp.where(lanes < (j + 1) * 128, s_ref[j, :, 0:512], 0.0)
            z_ref[...] += mm(inverse, s_ref[j, :, 512:640], 0, 0)
        return 0

    if z_ref is not None:
        z_ref[...] = jnp.zeros_like(z_ref)
    lax.fori_loop(0, 4, step, 0)


def pick(condition):
    return jnp.where(condition, jnp.float32(1.0), jnp.float32(0.0))


def row_coefficients(maps, child, quarter):
    entries = [maps[t, quarter, child] for t in range(7)]
    same = [pick(entries[p] == p) if p < 7 else None for p in range(8)]
    above = [pick(entries[p - 1] == p) if p > 0 else None for p in range(8)]
    return same, above


def place(same, above, p, blocks):
    if p == 0:
        return blocks(0) * same[0]
    if p == 7:
        return blocks(6) * above[7]
    return blocks(p) * same[p] + blocks(p - 1) * above[p]


def kernel(
    update, own, maps, out,
    mine, theirs, own_mine, own_theirs, tile1, s1, a1, v_mine, v_theirs, z, x, u, head_mine, head_theirs, tile2, s2, a2, zero,
    local, ex_s, ex_r, b1_s, b1_r, zx_s, zx_r, f1_s, f1_r, w1_s, w1_r, a1_s, a1_r, f2_s, f2_r, w2_s, w2_r, a2_s, a2_r, t_s, t_r,
):
    leaf, r, c = lax.axis_index("leaf"), lax.axis_index("frow"), lax.axis_index("fcol")
    core = lax.rem(leaf, 2)
    twin = leaf + 1 - 2 * core
    pair = leaf // 2
    other = pair + 1 - 2 * lax.rem(pair, 2)
    far = other * 2 + core
    cc, rc = pl.multiple_of(c * 128, 128), pl.multiple_of(r * 128, 128)
    h, g = pl.multiple_of(core * HALF, HALF), pl.multiple_of(HALF - core * HALF, HALF)
    upper = r <= c
    plane = [(i, j) for i in range(4) for j in range(4) if (i, j) != (0, 0)]

    def at(i, j):
        return {"frow": lax.rem(r + i, 4), "fcol": lax.rem(c + j, 4)}

    def send(src, dst, s, t, to):
        return pltpu.make_async_remote_copy(
            src_ref=src, dst_ref=dst, send_sem=s, recv_sem=t, device_id=to, device_id_type=MESH
        )

    loads = [
        pltpu.make_async_copy(update.at[pl.ds(0, 1), pl.ds(h, HALF), pl.ds(0, 256)], mine.at[pl.ds(0, 1)], local.at[0]),
        pltpu.make_async_copy(own.at[:, pl.ds(h, HALF), :], own_mine, local.at[1]),
        pltpu.make_async_copy(update.at[pl.ds(1, 6), pl.ds(h, HALF), pl.ds(0, 256)], mine.at[pl.ds(1, 6)], local.at[2]),
    ]
    for copy in loads:
        copy.start()

    barrier = pltpu.get_barrier_semaphore()
    pl.semaphore_signal(barrier, inc=1, device_id={"leaf": twin}, device_id_type=MESH)
    for i, j in plane:
        pl.semaphore_signal(barrier, inc=1, device_id=at(i, j), device_id_type=MESH)
    pl.semaphore_signal(barrier, inc=1, device_id={"leaf": far}, device_id_type=MESH)
    zero[...] = jnp.zeros_like(zero)
    pl.semaphore_wait(barrier, 17)

    swaps = [
        send(
            update.at[pl.ds(0, 1), pl.ds(g, HALF), pl.ds(0, 256)], theirs.at[pl.ds(0, 1)],
            ex_s.at[0], ex_r.at[0], {"leaf": twin},
        ),
        send(own.at[:, pl.ds(g, HALF), :], own_theirs, ex_s.at[1], ex_r.at[1], {"leaf": twin}),
        send(
            update.at[pl.ds(1, 6), pl.ds(g, HALF), pl.ds(0, 256)], theirs.at[pl.ds(1, 6)],
            ex_s.at[2], ex_r.at[2], {"leaf": twin},
        ),
    ]
    for copy in swaps:
        copy.start()

    sides = []
    for ref, child in ((mine, leaf), (theirs, twin)):
        same, above = row_coefficients(maps, child, r)
        first, second = maps[0, c, child], maps[1, c, child]
        sides.append((ref, same, above, pick(first == 0), pick(first == 1), pick(second == 1)))

    def front1(p, column):
        total = None
        for ref, same, above, none, one, two in sides:

            def blocks(t):
                left = ref[t, :, 0:128]
                if column == 0:
                    return left * none
                return left * one + ref[t, :, 128:256] * two

            part = place(same, above, p, blocks)
            total = part if total is None else total + part
        return total

    def spread(tile, store, s, t):
        return [
            send(tile, store.at[r, pl.ds(h, HALF), pl.ds(cc, 128)], s.at[4 * i + j], t.at[4 * r + c], at(i, j))
            for i, j in plane
        ]

    def start_spread(copies):
        @pl.when(upper)
        def _():
            for copy in copies:
                copy.start()

    def finish_spread(copies):
        @pl.when(upper)
        def _():
            for copy in copies:
                copy.wait_send()

    def arrived(tile, store, s, t, i, j):
        @pl.when(jnp.logical_or(r != i, c != j))
        def _():
            send(
                tile, store.at[i, pl.ds(h, HALF), pl.ds(128 * j, 128)], s.at[4 * i + j], t.at[4 * i + j], at(0, 1)
            ).wait_recv()

    def twin_parts(store, s, t, width, offset):
        bounds = [(0, 0, 128), (0, 128, width), (1, 128, width), (2, 256, width), (3, 384, width)]
        copies = []
        for n, (i, lo, hi) in enumerate(bounds):
            part = store.at[i, pl.ds(offset, HALF), pl.ds(lo, hi - lo)]
            copies.append(send(part, part, s.at[n], t.at[n], {"leaf": twin}))
        return copies

    def rows_out(store, s, t):
        block = store.at[:, pl.ds(cc, 128)]
        return [send(block, block, s.at[j], t.at[j], at(0, j)) for j in range(1, 4)]

    def rows_in(store, s, t):
        copies = []
        for j in range(1, 4):
            block = store.at[:, pl.ds(pl.multiple_of(lax.rem(c + 4 - j, 4) * 128, 128), 128)]
            copies.append(send(block, block, s.at[j], t.at[j], at(0, j)))
        return copies

    loads[0].wait()
    loads[1].wait()
    swaps[0].wait_recv()
    swaps[1].wait_recv()
    pivot = front1(0, 0) + (own_mine[0] + own_theirs[0])
    tile1[0] = pivot
    out1 = spread(tile1.at[0], s1, f1_s, f1_r)
    start_spread(out1)
    s1[r, pl.ds(h, HALF), pl.ds(cc, 128)] = pivot
    side = front1(0, 1)
    tile1[1] = side
    side1 = [
        send(tile1.at[1], s1.at[r, pl.ds(h, HALF), pl.ds(512, 128)], b1_s.at[i], b1_r.at[i], at(i, 0)) for i in range(1, 4)
    ]
    for copy in side1:
        copy.start()
    s1[r, pl.ds(h, HALF), pl.ds(512, 128)] = side

    loads[2].wait()
    swaps[2].wait_recv()
    for p in range(1, 8):
        a1[HALF * (p - 1):HALF * p, pl.ds(cc, 128)] = front1(p, 0)
        v_mine[HALF * (p - 1):HALF * p, :] = front1(p, 1)
    rows1 = rows_out(a1, a1_s, a1_r)

    def begin(tile, store, s, t, parts):
        arrived(tile, store, s, t, 0, 0)
        give, take = parts
        give[0].start()
        take[0].wait_recv()

    def middle_of(tile, store, s, t, parts, rest):
        def middle(j):
            @pl.when(j == 0)
            def _():
                for i in range(4):
                    for k in range(max(i, 1), 4):
                        arrived(tile, store, s, t, i, k)
                rest()
                for copy in parts[0][1:]:
                    copy.start()

        return middle

    def after_of(parts):
        def after(j):
            @pl.when(j == 0)
            def _():
                for copy in parts[1][1:]:
                    copy.wait_recv()
                for copy in parts[0]:
                    copy.wait_send()

        return after

    def nothing(j):
        return None

    def side_in_rows_out():
        for i in range(1, 4):
            send(
                tile1.at[1], s1.at[lax.rem(r + 4 - i, 4), pl.ds(h, HALF), pl.ds(512, 128)], b1_s.at[i], b1_r.at[i], at(i, 0)
            ).wait_recv()
        for copy in rows1:
            copy.start()

    parts1 = twin_parts(s1, w1_s, w1_r, 640, h), twin_parts(s1, w1_s, w1_r, 640, g)
    begin(tile1.at[0], s1, f1_s, f1_r, parts1)
    block_factor(
        s1, x, None, z, zero, nothing, middle_of(tile1.at[0], s1, f1_s, f1_r, parts1, side_in_rows_out), after_of(parts1)
    )
    for copy in rows_in(a1, a1_s, a1_r):
        copy.wait_recv()

    sides2 = []
    for child, ref in ((32 + pair, v_mine), (32 + other, v_theirs)):
        same, above = row_coefficients(maps, child, r)
        sides2.append((ref, same, above, pick(maps[0, c, child] == 0)))

    v_mine[0:HALF, :] = v_mine[0:HALF, :] - mm(a1[0:HALF, :], z[...], 1, 0)
    _, same, _, first = sides2[0]
    head_mine[...] = v_mine[0:HALF, :] * same[0] * first + (own_mine[1] + own_theirs[1])
    head = send(head_mine, head_theirs, zx_s.at[0], zx_r.at[0], {"leaf": far})
    head.start()
    v_mine[HALF:, :] = v_mine[HALF:, :] - mm(a1[HALF:, :], z[...], 1, 0)
    rest = send(v_mine, v_theirs, zx_s.at[1], zx_r.at[1], {"leaf": far})
    rest.start()

    head.wait_recv()
    pivot = head_mine[...] + head_theirs[...]
    tile2[...] = pivot
    out2 = spread(tile2, s2, f2_s, f2_r)
    start_spread(out2)
    s2[r, pl.ds(h, HALF), pl.ds(cc, 128)] = pivot
    rest.wait_recv()
    a2_own = a2.at[core]
    for p in range(1, 8):
        total = None
        for ref, same, above, first in sides2:
            part = place(same, above, p, lambda t: ref[HALF * t:HALF * t + HALF, :]) * first
            total = part if total is None else total + part
        a2[core, HALF * (p - 1):HALF * p, pl.ds(cc, 128)] = total
    rows2 = rows_out(a2_own, a2_s, a2_r)

    def rows_out2():
        for copy in rows2:
            copy.start()

    a2_give = send(a2_own, a2_own, t_s.at[0], t_r.at[0], {"leaf": twin})
    a2_twin = a2.at[1 - core]
    a2_take = send(a2_twin, a2_twin, t_s.at[0], t_r.at[0], {"leaf": twin})

    def before2(j):
        @pl.when(j == 3)
        def _():
            for copy in rows_in(a2_own, a2_s, a2_r):
                copy.wait_recv()
            a2_give.start()

    parts2 = twin_parts(s2, w2_s, w2_r, 512, h), twin_parts(s2, w2_s, w2_r, 512, g)
    begin(tile2, s2, f2_s, f2_r, parts2)
    block_factor(s2, x, u, None, zero, before2, middle_of(tile2, s2, f2_s, f2_r, parts2, rows_out2), after_of(parts2))

    lanes = lax.broadcasted_iota(jnp.int32, (128, 512), 1)
    inverse = jnp.where(lanes < (c + 1) * 128, s2[c], 0.0)

    def lower_rows(k):
        result = mm(a2[k], inverse, 1, 1)
        k0 = pl.multiple_of(k * HALF, HALF)
        for p in range(7):
            out[p + 1, pl.ds(k0, HALF), :] = result[HALF * p:HALF * p + HALF, :]

    lower_rows(core)
    r_i = lax.broadcasted_iota(jnp.int32, (128, 128), 0)
    c_i = lax.broadcasted_iota(jnp.int32, (128, 128), 1)
    corner = jnp.where(r_i >= c_i, mm(u[c], s2[c, :, pl.ds(cc, 128)], 1, 1), 0.0)
    out[0] = s2[c, :, pl.ds(rc, 128)].T * pick(r > c) + corner * pick(r == c)
    a2_take.wait_recv()
    lower_rows(1 - core)
    a2_give.wait_send()
    for copy in swaps + side1 + rows1 + [head, rest] + rows2:
        copy.wait_send()
    finish_spread(out1)
    finish_spread(out2)


def on_device(child_update, own_part, child_maps):
    shapes = [
        (7, 64, 256), (7, 64, 256), (2, 64, 128), (2, 64, 128), (2, 64, 128), (4, 128, 640), (448, 512), (448, 128), (448, 128),
        (512, 128), (128, 128), (4, 128, 128), (64, 128), (64, 128), (64, 128), (4, 128, 512), (2, 448, 512), (8, 128),
    ]
    sems = [3, 3, 3, 4, 4, 2, 2] + [16, 16, 5, 5, 4, 4] * 2 + [1, 1]
    panel = pl.pallas_call(
        kernel,
        out_shape=jax.ShapeDtypeStruct((8, 128, 128), jnp.float32),
        in_specs=[
            pl.BlockSpec(memory_space=pl.ANY),
            pl.BlockSpec(memory_space=pl.ANY),
            pl.BlockSpec(memory_space=pltpu.SMEM),
        ],
        out_specs=pl.BlockSpec(memory_space=pltpu.VMEM),
        scratch_shapes=[pltpu.VMEM(s, jnp.float32) for s in shapes] + [pltpu.SemaphoreType.DMA((n,)) for n in sems],
        compiler_params=pltpu.CompilerParams(collective_id=0, has_side_effects=True, vmem_limit_bytes=62 << 20),
        name="merge",
    )(child_update[0].reshape(7, 128, 896), own_part[0], child_maps.transpose(2, 1, 0))
    return panel.reshape(1, 1024, 128)


def solution(mesh):
    in_specs = (P("leaf", "frow", "fcol"), P("leaf", None, "frow", "fcol"), P())
    out_specs = P("leaf", "frow", "fcol")
    return jax.shard_map(on_device, mesh=mesh, in_specs=in_specs, out_specs=out_specs, check_vma=False)
```

time: 108 us -> 70.4 us (0.65)
  Pallas kernels: 103 us -> 68.3 us
  local copies, waits for them, and re-layouts: 4.43 us -> 1.87 us
    pallas_call x1, Pallas kernels: 103 us -> 68.3 us  [on_device(): pl.pallas_call(kernel, out_shape=jax.ShapeDtypeStruct((8, 128, 128), jnp....]
    unnamed x6 -> x1, local copies, waits for them, and re-layouts: 4.43 us -> 1.87 us
where the time goes in v2:
time: 70.4 us; the launch traced here: 70.2 us
  Pallas kernels  68.3 us (97%)
  local copies, waits for them, and re-layouts  1.87 us (3%)
    pallas_call x1, Pallas kernels, on_device(): pl.pallas_call(kernel, out_shape=jax.ShapeDtypeStruct((8, 128, 128), jnp....  68.3 us
    unnamed x1, local copies, waits for them, and re-layouts  1.87 us

profile of v2, /device:TPU:1, one launch (start us, length us, event | category | flops | bytes accessed | tf_op | source)
XLA Modules:
  0.0 70.2 jit_solution(4054232940254278595)
XLA Ops:
  0.0 68.3 %merge.1 = f32[8,128,128]{2,1,0:T(8,128)} custom-call(f32[7,128,896]{2,1,0:T(8,128)} %bitcast.4, f32[2,128,128]{2,1,0:T(8,128)} %bitcast.6, s32[7,4,48]{2,1,0:T(4,128)} %bitcast.7), custom_call_target="tpu_custom_call" | custom-call | tf_op jit(solution)/shard_map/merge/pallas_call | solution.py:403
  68.3 1.9 %copy.5 = f32[1,1024,128]{2,1,0:T(8,128)} copy(f32[1,1024,128]{2,1,0:T(8,128)} %bitcast.5) | data formatting | bytes 1048576

commit v3 on v2

--- a/solution.py
+++ b/solution.py
@@ -5,13 +5,29 @@
 from jax.experimental.pallas import tpu as pltpu
 from jax.sharding import PartitionSpec as P
 
-HI = lax.Precision.HIGHEST
 MESH = pl.DeviceIdType.MESH
 HALF = 64
 
 
-def mm(a, b, ca, cb):
-    return lax.dot_general(a, b, (((ca,), (cb,)), ((), ())), precision=HI, preferred_element_type=jnp.float32)
+def thirds(v):
+    high = v.astype(jnp.bfloat16)
+    rest = v - high.astype(jnp.float32)
+    middle = rest.astype(jnp.bfloat16)
+    return high, middle, (rest - middle.astype(jnp.float32)).astype(jnp.bfloat16)
+
+
+def left(v):
+    h, m, l = thirds(v)
+    return jnp.concatenate([h, h, m, h, m, l], 1)
+
+
+def right(v):
+    h, m, l = thirds(v)
+    return jnp.concatenate([h, m, h, l, m, h], 0)
+
+
+def dot(a, b):
+    return lax.dot_general(a, b, (((1,), (0,)), ((), ())), preferred_element_type=jnp.float32)
 
 
 def spread_column(v, j):
@@ -78,7 +94,7 @@
         x_ref[base:base + 8, :] = jnp.where(lane < base + 8, done, 0.0)
 
 
-def block_factor(s_ref, x_ref, u_ref, z_ref, zero_ref, before, middle, after):
+def block_factor(s_ref, x_ref, u_ref, z_ref, zero_ref, before, middle, after, later):
     def step(j, _):
         cj = pl.multiple_of(j * 128, 128)
         before(j)
@@ -91,19 +107,22 @@
         r_i = lax.broadcasted_iota(jnp.int32, (128, 128), 0)
         c_i = lax.broadcasted_iota(jnp.int32, (128, 128), 1)
         s_ref[j, :, pl.ds(cj, 128)] = (r_i == c_i).astype(jnp.float32)
-        s_ref[j] = mm(x_ref[...], s_ref[j], 1, 0)
+        u = dot(left(x_ref[...]), right(s_ref[j]))
+        s_ref[j] = u
+        later(j)
+        u = right(u)
 
         def trail(i, _):
             ci = pl.multiple_of(i * 128, 128)
             s_ref[i, :, pl.ds(cj, 128)] = jnp.zeros((128, 128), jnp.float32)
-            s_ref[i] = s_ref[i] - mm(s_ref[j, :, pl.ds(ci, 128)], s_ref[j], 0, 0)
+            s_ref[i] = s_ref[i] - dot(left(s_ref[j, :, pl.ds(ci, 128)].T), u)
             return 0
 
         lax.fori_loop(j + 1, 4, trail, 0)
         if z_ref is not None:
             lanes = lax.broadcasted_iota(jnp.int32, (128, 512), 1)
             inverse = jnp.where(lanes < (j + 1) * 128, s_ref[j, :, 0:512], 0.0)
-            z_ref[...] += mm(inverse, s_ref[j, :, 512:640], 0, 0)
+            z_ref[...] += dot(left(inverse.T), u[:, 512:640])
         return 0
 
     if z_ref is not None:
@@ -131,8 +150,8 @@
 
 
 def kernel(
-    update, own, maps, out,
-    mine, theirs, own_mine, own_theirs, tile1, s1, a1, v_mine, v_theirs, z, x, u, head_mine, head_theirs, tile2, s2, a2, zero,
+    update, own, maps_in, out,
+    mine, theirs, own_mine, own_theirs, tile1, s1, a1, v_mine, v_theirs, z, x, u, head_mine, head_theirs, tile2, s2, a2, zero, maps,
     local, ex_s, ex_r, b1_s, b1_r, zx_s, zx_r, f1_s, f1_r, w1_s, w1_r, a1_s, a1_r, f2_s, f2_r, w2_s, w2_r, a2_s, a2_r, t_s, t_r,
 ):
     leaf, r, c = lax.axis_index("leaf"), lax.axis_index("frow"), lax.axis_index("fcol")
@@ -143,7 +162,7 @@
     far = other * 2 + core
     cc, rc = pl.multiple_of(c * 128, 128), pl.multiple_of(r * 128, 128)
     h, g = pl.multiple_of(core * HALF, HALF), pl.multiple_of(HALF - core * HALF, HALF)
-    upper = r <= c
+    upper = jnp.logical_or(jnp.logical_and(r <= c, c - r < 3), r - c == 3)
     plane = [(i, j) for i in range(4) for j in range(4) if (i, j) != (0, 0)]
 
     def at(i, j):
@@ -157,6 +176,7 @@
     loads = [
         pltpu.make_async_copy(update.at[pl.ds(0, 1), pl.ds(h, HALF), pl.ds(0, 256)], mine.at[pl.ds(0, 1)], local.at[0]),
         pltpu.make_async_copy(own.at[:, pl.ds(h, HALF), :], own_mine, local.at[1]),
+        pltpu.make_async_copy(maps_in, maps, local.at[3]),
         pltpu.make_async_copy(update.at[pl.ds(1, 6), pl.ds(h, HALF), pl.ds(0, 256)], mine.at[pl.ds(1, 6)], local.at[2]),
     ]
     for copy in loads:
@@ -184,6 +204,7 @@
     for copy in swaps:
         copy.start()
 
+    loads[2].wait()
     sides = []
     for ref, child in ((mine, leaf), (theirs, twin)):
         same, above = row_coefficients(maps, child, r)
@@ -230,7 +251,9 @@
             ).wait_recv()
 
     def twin_parts(store, s, t, width, offset):
-        bounds = [(0, 0, 128), (0, 128, width), (1, 128, width), (2, 256, width), (3, 384, width)]
+        bounds = [(0, 0, 128), (0, 128, 384), (3, 0, 128), (1, 128, width), (2, 256, width), (3, 384, width)]
+        if width > 512:
+            bounds.insert(2, (0, 512, width))
         copies = []
         for n, (i, lo, hi) in enumerate(bounds):
             part = store.at[i, pl.ds(offset, HALF), pl.ds(lo, hi - lo)]
@@ -266,7 +289,7 @@
         copy.start()
     s1[r, pl.ds(h, HALF), pl.ds(512, 128)] = side
 
-    loads[2].wait()
+    loads[3].wait()
     swaps[2].wait_recv()
     for p in range(1, 8):
         a1[HALF * (p - 1):HALF * p, pl.ds(cc, 128)] = front1(p, 0)
@@ -283,25 +306,35 @@
         def middle(j):
             @pl.when(j == 0)
             def _():
-                for i in range(4):
-                    for k in range(max(i, 1), 4):
-                        arrived(tile, store, s, t, i, k)
+                for i, k in ((0, 1), (0, 2), (3, 0), (1, 1), (1, 2), (1, 3), (2, 2), (2, 3), (3, 3)):
+                    arrived(tile, store, s, t, i, k)
                 rest()
                 for copy in parts[0][1:]:
                     copy.start()
 
         return middle
 
-    def after_of(parts):
+    def after_of(store, parts):
+        head = len(parts[0]) - 3
+
         def after(j):
             @pl.when(j == 0)
             def _():
-                for copy in parts[1][1:]:
+                for copy in parts[1][1:head]:
                     copy.wait_recv()
-                for copy in parts[0]:
+                for copy in parts[0][:head]:
                     copy.wait_send()
-
-        return after
+                store[0, :, 384:512] = store[3, :, 0:128].T
+
+        def later(j):
+            @pl.when(j == 0)
+            def _():
+                for copy in parts[1][head:]:
+                    copy.wait_recv()
+                for copy in parts[0][head:]:
+                    copy.wait_send()
+
+        return after, later
 
     def nothing(j):
         return None
@@ -317,7 +350,7 @@
     parts1 = twin_parts(s1, w1_s, w1_r, 640, h), twin_parts(s1, w1_s, w1_r, 640, g)
     begin(tile1.at[0], s1, f1_s, f1_r, parts1)
     block_factor(
-        s1, x, None, z, zero, nothing, middle_of(tile1.at[0], s1, f1_s, f1_r, parts1, side_in_rows_out), after_of(parts1)
+        s1, x, None, z, zero, nothing, middle_of(tile1.at[0], s1, f1_s, f1_r, parts1, side_in_rows_out), *after_of(s1, parts1)
     )
     for copy in rows_in(a1, a1_s, a1_r):
         copy.wait_recv()
@@ -327,12 +360,13 @@
         same, above = row_coefficients(maps, child, r)
         sides2.append((ref, same, above, pick(maps[0, c, child] == 0)))
 
-    v_mine[0:HALF, :] = v_mine[0:HALF, :] - mm(a1[0:HALF, :], z[...], 1, 0)
+    z_right = right(z[...])
+    v_mine[0:HALF, :] = v_mine[0:HALF, :] - dot(left(a1[0:HALF, :]), z_right)
     _, same, _, first = sides2[0]
     head_mine[...] = v_mine[0:HALF, :] * same[0] * first + (own_mine[1] + own_theirs[1])
     head = send(head_mine, head_theirs, zx_s.at[0], zx_r.at[0], {"leaf": far})
     head.start()
-    v_mine[HALF:, :] = v_mine[HALF:, :] - mm(a1[HALF:, :], z[...], 1, 0)
+    v_mine[HALF:, :] = v_mine[HALF:, :] - dot(left(a1[HALF:, :]), z_right)
     rest = send(v_mine, v_theirs, zx_s.at[1], zx_r.at[1], {"leaf": far})
     rest.start()
 
@@ -369,13 +403,13 @@
 
     parts2 = twin_parts(s2, w2_s, w2_r, 512, h), twin_parts(s2, w2_s, w2_r, 512, g)
     begin(tile2, s2, f2_s, f2_r, parts2)
-    block_factor(s2, x, u, None, zero, before2, middle_of(tile2, s2, f2_s, f2_r, parts2, rows_out2), after_of(parts2))
+    block_factor(s2, x, u, None, zero, before2, middle_of(tile2, s2, f2_s, f2_r, parts2, rows_out2), *after_of(s2, parts2))
 
     lanes = lax.broadcasted_iota(jnp.int32, (128, 512), 1)
-    inverse = jnp.where(lanes < (c + 1) * 128, s2[c], 0.0)
+    inverse = right(jnp.where(lanes < (c + 1) * 128, s2[c], 0.0).T)
 
     def lower_rows(k):
-        result = mm(a2[k], inverse, 1, 1)
+        result = dot(left(a2[k]), inverse)
         k0 = pl.multiple_of(k * HALF, HALF)
         for p in range(7):
             out[p + 1, pl.ds(k0, HALF), :] = result[HALF * p:HALF * p + HALF, :]
@@ -383,7 +417,7 @@
     lower_rows(core)
     r_i = lax.broadcasted_iota(jnp.int32, (128, 128), 0)
     c_i = lax.broadcasted_iota(jnp.int32, (128, 128), 1)
-    corner = jnp.where(r_i >= c_i, mm(u[c], s2[c, :, pl.ds(cc, 128)], 1, 1), 0.0)
+    corner = jnp.where(r_i >= c_i, dot(left(u[c]), right(s2[c, :, pl.ds(cc, 128)].T)), 0.0)
     out[0] = s2[c, :, pl.ds(rc, 128)].T * pick(r > c) + corner * pick(r == c)
     a2_take.wait_recv()
     lower_rows(1 - core)
@@ -399,17 +433,19 @@
         (7, 64, 256), (7, 64, 256), (2, 64, 128), (2, 64, 128), (2, 64, 128), (4, 128, 640), (448, 512), (448, 128), (448, 128),
         (512, 128), (128, 128), (4, 128, 128), (64, 128), (64, 128), (64, 128), (4, 128, 512), (2, 448, 512), (8, 128),
     ]
-    sems = [3, 3, 3, 4, 4, 2, 2] + [16, 16, 5, 5, 4, 4] * 2 + [1, 1]
+    sems = [4, 3, 3, 4, 4, 2, 2] + [16, 16, 7, 7, 4, 4] * 2 + [1, 1]
     panel = pl.pallas_call(
         kernel,
         out_shape=jax.ShapeDtypeStruct((8, 128, 128), jnp.float32),
         in_specs=[
             pl.BlockSpec(memory_space=pl.ANY),
             pl.BlockSpec(memory_space=pl.ANY),
-            pl.BlockSpec(memory_space=pltpu.SMEM),
+            pl.BlockSpec(memory_space=pl.ANY),
         ],
         out_specs=pl.BlockSpec(memory_space=pltpu.VMEM),
-        scratch_shapes=[pltpu.VMEM(s, jnp.float32) for s in shapes] + [pltpu.SemaphoreType.DMA((n,)) for n in sems],
+        scratch_shapes=[pltpu.VMEM(s, jnp.float32) for s in shapes]
+        + [pltpu.SMEM((7, 4, 48), jnp.int32)]
+        + [pltpu.SemaphoreType.DMA((n,)) for n in sems],
         compiler_params=pltpu.CompilerParams(collective_id=0, has_side_effects=True, vmem_limit_bytes=62 << 20),
         name="merge",
     )(child_update[0].reshape(7, 128, 896), own_part[0], child_maps.transpose(2, 1, 0))

time: 70.4 us -> 68.3 us (0.970)
  Pallas kernels: 68.3 us -> 65.9 us
    pallas_call x1, Pallas kernels: 68.3 us -> 65.9 us  [on_device(): pl.pallas_call(kernel, out_shape=jax.ShapeDtypeStruct((8, 128, 128), jnp....]
where the time goes in v3:
time: 68.3 us; the launch traced here: 67.8 us
  Pallas kernels  65.9 us (96%)
  local copies, waits for them, and re-layouts  1.87 us (3%)
    pallas_call x1, Pallas kernels, on_device(): pl.pallas_call(kernel, out_shape=jax.ShapeDtypeStruct((8, 128, 128), jnp....  65.9 us
    unnamed x1, local copies, waits for them, and re-layouts  1.87 us

profile of v3, /device:TPU:1, one launch (start us, length us, event | category | flops | bytes accessed | tf_op | source)
XLA Modules:
  0.0 67.8 jit_solution(12503964481671172202)
XLA Ops:
  0.0 65.9 %merge.1 = f32[8,128,128]{2,1,0:T(8,128)} custom-call(f32[7,128,896]{2,1,0:T(8,128)} %bitcast.4, f32[2,128,128]{2,1,0:T(8,128)} %bitcast.6, s32[7,4,48]{2,1,0:T(4,128)} %bitcast.7), custom_call_target="tpu_custom_call" | custom-call | tf_op jit(solution)/shard_map/merge/pallas_call | solution.py:437
  66.0 1.9 %copy.5 = f32[1,1024,128]{2,1,0:T(8,128)} copy(f32[1,1024,128]{2,1,0:T(8,128)} %bitcast.5) | data formatting | bytes 1048576

commit v4 on v3

--- a/solution.py
+++ b/solution.py
@@ -151,7 +151,7 @@
 
 def kernel(
     update, own, maps_in, out,
-    mine, theirs, own_mine, own_theirs, tile1, s1, a1, v_mine, v_theirs, z, x, u, head_mine, head_theirs, tile2, s2, a2, zero, maps,
+    mine, theirs, own_mine, own_theirs, tile1, s1, a1, v_mine, v_theirs, z, x, u, head_mine, head_theirs, tile2, s2, a2, zero, land1, land2, maps,
     local, ex_s, ex_r, b1_s, b1_r, zx_s, zx_r, f1_s, f1_r, w1_s, w1_r, a1_s, a1_r, f2_s, f2_r, w2_s, w2_r, a2_s, a2_r, t_s, t_r,
 ):
     leaf, r, c = lax.axis_index("leaf"), lax.axis_index("frow"), lax.axis_index("fcol")
@@ -163,6 +163,8 @@
     cc, rc = pl.multiple_of(c * 128, 128), pl.multiple_of(r * 128, 128)
     h, g = pl.multiple_of(core * HALF, HALF), pl.multiple_of(HALF - core * HALF, HALF)
     upper = jnp.logical_or(jnp.logical_and(r <= c, c - r < 3), r - c == 3)
+    early = jnp.logical_or(jnp.logical_and(r == 0, c < 3), r - c == 3)
+    late = jnp.logical_and(upper, jnp.logical_not(early))
     plane = [(i, j) for i in range(4) for j in range(4) if (i, j) != (0, 0)]
 
     def at(i, j):
@@ -187,7 +189,8 @@
     for i, j in plane:
         pl.semaphore_signal(barrier, inc=1, device_id=at(i, j), device_id_type=MESH)
     pl.semaphore_signal(barrier, inc=1, device_id={"leaf": far}, device_id_type=MESH)
-    zero[...] = jnp.zeros_like(zero)
+    for ref in (zero, s1, s2):
+        ref[...] = jnp.zeros_like(ref)
     pl.semaphore_wait(barrier, 17)
 
     swaps = [
@@ -231,8 +234,8 @@
             for i, j in plane
         ]
 
-    def start_spread(copies):
-        @pl.when(upper)
+    def start_spread(copies, when):
+        @pl.when(when)
         def _():
             for copy in copies:
                 copy.start()
@@ -277,81 +280,103 @@
     swaps[1].wait_recv()
     pivot = front1(0, 0) + (own_mine[0] + own_theirs[0])
     tile1[0] = pivot
-    out1 = spread(tile1.at[0], s1, f1_s, f1_r)
-    start_spread(out1)
-    s1[r, pl.ds(h, HALF), pl.ds(cc, 128)] = pivot
+    out1 = spread(tile1.at[0], land1, f1_s, f1_r)
+    start_spread(out1, early)
+    land1[r, pl.ds(h, HALF), pl.ds(cc, 128)] = pivot
     side = front1(0, 1)
     tile1[1] = side
     side1 = [
-        send(tile1.at[1], s1.at[r, pl.ds(h, HALF), pl.ds(512, 128)], b1_s.at[i], b1_r.at[i], at(i, 0)) for i in range(1, 4)
+        send(tile1.at[1], land1.at[r, pl.ds(h, HALF), pl.ds(512, 128)], b1_s.at[i], b1_r.at[r], at(i, 0)) for i in range(1, 4)
     ]
-    for copy in side1:
-        copy.start()
-    s1[r, pl.ds(h, HALF), pl.ds(512, 128)] = side
+    start_spread(side1, r == 0)
+    land1[r, pl.ds(h, HALF), pl.ds(512, 128)] = side
 
     loads[3].wait()
     swaps[2].wait_recv()
     for p in range(1, 8):
         a1[HALF * (p - 1):HALF * p, pl.ds(cc, 128)] = front1(p, 0)
         v_mine[HALF * (p - 1):HALF * p, :] = front1(p, 1)
+    start_spread(out1, late)
+    start_spread(side1, r > 0)
     rows1 = rows_out(a1, a1_s, a1_r)
 
-    def begin(tile, store, s, t, parts):
-        arrived(tile, store, s, t, 0, 0)
+    def hooks(tile, store, sums, s, t, parts, width, side_arrived, rest):
         give, take = parts
-        give[0].start()
-        take[0].wait_recv()
-
-    def middle_of(tile, store, s, t, parts, rest):
+        head = len(give) - 3
+        groups = [((0, 1), (0, 2), (3, 0)), ((1, 1), (1, 2), (1, 3)), ((2, 2), (2, 3), (3, 3))]
+
+        def arrive(group):
+            for i, k in groups[group]:
+                arrived(tile, store, s, t, i, k)
+
+        def before(j):
+            @pl.when(j == 0)
+            def _():
+                arrived(tile, store, s, t, 0, 0)
+                give[0].start()
+                take[0].wait_recv()
+                sums[0, :, 0:128] = store[0, :, 0:128]
+
+            for i in range(1, 4):
+                def add(i=i):
+                    take[head + i - 1].wait_recv()
+                    sums[i, :, 128 * i:width] = sums[i, :, 128 * i:width] + store[i, :, 128 * i:width]
+
+                pl.when(j == i)(add)
+
         def middle(j):
             @pl.when(j == 0)
             def _():
-                for i, k in ((0, 1), (0, 2), (3, 0), (1, 1), (1, 2), (1, 3), (2, 2), (2, 3), (3, 3)):
-                    arrived(tile, store, s, t, i, k)
+                arrive(0)
+                side_arrived(0)
+                for copy in give[1:head]:
+                    copy.start()
                 rest()
-                for copy in parts[0][1:]:
+
+            @pl.when(j == 1)
+            def _():
+                arrive(2)
+                side_arrived(2)
+                side_arrived(3)
+                for copy in give[head + 1:]:
                     copy.start()
-
-        return middle
-
-    def after_of(store, parts):
-        head = len(parts[0]) - 3
 
         def after(j):
             @pl.when(j == 0)
             def _():
-                for copy in parts[1][1:head]:
+                for copy in take[1:head]:
                     copy.wait_recv()
-                for copy in parts[0][:head]:
-                    copy.wait_send()
-                store[0, :, 384:512] = store[3, :, 0:128].T
+                sums[0, :, 128:384] = store[0, :, 128:384]
+                sums[0, :, 384:512] = store[3, :, 0:128].T
+                if width > 512:
+                    sums[0, :, 512:width] = store[0, :, 512:width]
 
         def later(j):
             @pl.when(j == 0)
             def _():
-                for copy in parts[1][head:]:
-                    copy.wait_recv()
-                for copy in parts[0][head:]:
-                    copy.wait_send()
-
-        return after, later
-
-    def nothing(j):
+                arrive(1)
+                side_arrived(1)
+                give[head].start()
+
+        return before, middle, after, later
+
+    def side_arrived(i):
+        @pl.when(r != i)
+        def _():
+            send(
+                tile1.at[1], land1.at[i, pl.ds(h, HALF), pl.ds(512, 128)], b1_s.at[1], b1_r.at[i], at(1, 0)
+            ).wait_recv()
+
+    def nothing(i):
         return None
 
-    def side_in_rows_out():
-        for i in range(1, 4):
-            send(
-                tile1.at[1], s1.at[lax.rem(r + 4 - i, 4), pl.ds(h, HALF), pl.ds(512, 128)], b1_s.at[i], b1_r.at[i], at(i, 0)
-            ).wait_recv()
+    def rows_out1():
         for copy in rows1:
             copy.start()
 
-    parts1 = twin_parts(s1, w1_s, w1_r, 640, h), twin_parts(s1, w1_s, w1_r, 640, g)
-    begin(tile1.at[0], s1, f1_s, f1_r, parts1)
-    block_factor(
-        s1, x, None, z, zero, nothing, middle_of(tile1.at[0], s1, f1_s, f1_r, parts1, side_in_rows_out), *after_of(s1, parts1)
-    )
+    parts1 = twin_parts(land1, w1_s, w1_r, 640, h), twin_parts(land1, w1_s, w1_r, 640, g)
+    hooks1 = hooks(tile1.at[0], land1, s1, f1_s, f1_r, parts1, 640, side_arrived, rows_out1)
+    block_factor(s1, x, None, z, zero, *hooks1)
     for copy in rows_in(a1, a1_s, a1_r):
         copy.wait_recv()
 
@@ -373,9 +398,9 @@
     head.wait_recv()
     pivot = head_mine[...] + head_theirs[...]
     tile2[...] = pivot
-    out2 = spread(tile2, s2, f2_s, f2_r)
-    start_spread(out2)
-    s2[r, pl.ds(h, HALF), pl.ds(cc, 128)] = pivot
+    out2 = spread(tile2, land2, f2_s, f2_r)
+    start_spread(out2, upper)
+    land2[r, pl.ds(h, HALF), pl.ds(cc, 128)] = pivot
     rest.wait_recv()
     a2_own = a2.at[core]
     for p in range(1, 8):
@@ -394,16 +419,19 @@
     a2_twin = a2.at[1 - core]
     a2_take = send(a2_twin, a2_twin, t_s.at[0], t_r.at[0], {"leaf": twin})
 
-    def before2(j):
+    parts2 = twin_parts(land2, w2_s, w2_r, 512, h), twin_parts(land2, w2_s, w2_r, 512, g)
+    before2, middle2, after2, later2 = hooks(tile2, land2, s2, f2_s, f2_r, parts2, 512, nothing, rows_out2)
+
+    def middle2_rows(j):
+        middle2(j)
+
         @pl.when(j == 3)
         def _():
             for copy in rows_in(a2_own, a2_s, a2_r):
                 copy.wait_recv()
             a2_give.start()
 
-    parts2 = twin_parts(s2, w2_s, w2_r, 512, h), twin_parts(s2, w2_s, w2_r, 512, g)
-    begin(tile2, s2, f2_s, f2_r, parts2)
-    block_factor(s2, x, u, None, zero, before2, middle_of(tile2, s2, f2_s, f2_r, parts2, rows_out2), *after_of(s2, parts2))
+    block_factor(s2, x, u, None, zero, before2, middle2_rows, after2, later2)
 
     lanes = lax.broadcasted_iota(jnp.int32, (128, 512), 1)
     inverse = right(jnp.where(lanes < (c + 1) * 128, s2[c], 0.0).T)
@@ -422,7 +450,7 @@
     a2_take.wait_recv()
     lower_rows(1 - core)
     a2_give.wait_send()
-    for copy in swaps + side1 + rows1 + [head, rest] + rows2:
+    for copy in swaps + side1 + rows1 + [head, rest] + rows2 + parts1[0] + parts2[0]:
         copy.wait_send()
     finish_spread(out1)
     finish_spread(out2)
@@ -432,6 +460,7 @@
     shapes = [
         (7, 64, 256), (7, 64, 256), (2, 64, 128), (2, 64, 128), (2, 64, 128), (4, 128, 640), (448, 512), (448, 128), (448, 128),
         (512, 128), (128, 128), (4, 128, 128), (64, 128), (64, 128), (64, 128), (4, 128, 512), (2, 448, 512), (8, 128),
+        (4, 128, 640), (4, 128, 512),
     ]
     sems = [4, 3, 3, 4, 4, 2, 2] + [16, 16, 7, 7, 4, 4] * 2 + [1, 1]
     panel = pl.pallas_call(

time: 68.3 us -> 66.8 us (0.978)
  the two profiles are of different devices: /device:TPU:1 before, /device:TPU:5 now
where the time goes in v4:
time: 66.8 us; the launch traced here: 66.6 us
  Pallas kernels  64.7 us (97%)
  local copies, waits for them, and re-layouts  1.87 us (3%)
    pallas_call x1, Pallas kernels, on_device(): pl.pallas_call(kernel, out_shape=jax.ShapeDtypeStruct((8, 128, 128), jnp....  64.7 us
    unnamed x1, local copies, waits for them, and re-layouts  1.87 us

profile of v4, /device:TPU:5, one launch (start us, length us, event | category | flops | bytes accessed | tf_op | source)
XLA Modules:
  0.0 66.6 jit_solution(17483424529111264587)
XLA Ops:
  0.0 64.7 %merge.1 = f32[8,128,128]{2,1,0:T(8,128)} custom-call(f32[7,128,896]{2,1,0:T(8,128)} %bitcast.4, f32[2,128,128]{2,1,0:T(8,128)} %bitcast.6, s32[7,4,48]{2,1,0:T(4,128)} %bitcast.7), custom_call_target="tpu_custom_call" | custom-call | tf_op jit(solution)/shard_map/merge/pallas_call | solution.py:466
  64.7 1.9 %copy.5 = f32[1,1024,128]{2,1,0:T(8,128)} copy(f32[1,1024,128]{2,1,0:T(8,128)} %bitcast.5) | data formatting | bytes 1048576

commit v5 on v4

--- a/solution.py
+++ b/solution.py
@@ -165,7 +165,7 @@
     upper = jnp.logical_or(jnp.logical_and(r <= c, c - r < 3), r - c == 3)
     early = jnp.logical_or(jnp.logical_and(r == 0, c < 3), r - c == 3)
     late = jnp.logical_and(upper, jnp.logical_not(early))
-    plane = [(i, j) for i in range(4) for j in range(4) if (i, j) != (0, 0)]
+    plane = [(i, j) for i in (2, 1, 3, 0) for j in (2, 1, 3, 0) if (i, j) != (0, 0)]
 
     def at(i, j):
         return {"frow": lax.rem(r + i, 4), "fcol": lax.rem(c + j, 4)}
@@ -422,8 +422,8 @@
     parts2 = twin_parts(land2, w2_s, w2_r, 512, h), twin_parts(land2, w2_s, w2_r, 512, g)
     before2, middle2, after2, later2 = hooks(tile2, land2, s2, f2_s, f2_r, parts2, 512, nothing, rows_out2)
 
-    def middle2_rows(j):
-        middle2(j)
+    def before2_rows(j):
+        before2(j)
 
         @pl.when(j == 3)
         def _():
@@ -431,7 +431,7 @@
                 copy.wait_recv()
             a2_give.start()
 
-    block_factor(s2, x, u, None, zero, before2, middle2_rows, after2, later2)
+    block_factor(s2, x, u, None, zero, before2_rows, middle2, after2, later2)
 
     lanes = lax.broadcasted_iota(jnp.int32, (128, 512), 1)
     inverse = right(jnp.where(lanes < (c + 1) * 128, s2[c], 0.0).T)

time: 66.8 us -> 67.3 us (level)
  the two profiles are of different devices: /device:TPU:5 before, /device:TPU:67 now
where the time goes in v5:
time: 67.3 us; the launch traced here: 67.2 us
  Pallas kernels  65.3 us (97%)
  local copies, waits for them, and re-layouts  1.87 us (3%)
    pallas_call x1, Pallas kernels, on_device(): pl.pallas_call(kernel, out_shape=jax.ShapeDtypeStruct((8, 128, 128), jnp....  65.3 us
    unnamed x1, local copies, waits for them, and re-layouts  1.87 us

profile of v5, /device:TPU:67, one launch (start us, length us, event | category | flops | bytes accessed | tf_op | source)
XLA Modules:
  0.0 67.2 jit_solution(16426808879729155318)
XLA Ops:
  0.0 65.3 %merge.1 = f32[8,128,128]{2,1,0:T(8,128)} custom-call(f32[7,128,896]{2,1,0:T(8,128)} %bitcast.4, f32[2,128,128]{2,1,0:T(8,128)} %bitcast.6, s32[7,4,48]{2,1,0:T(4,128)} %bitcast.7), custom_call_target="tpu_custom_call" | custom-call | tf_op jit(solution)/shard_map/merge/pallas_call | solution.py:466
  65.3 1.9 %copy.5 = f32[1,1024,128]{2,1,0:T(8,128)} copy(f32[1,1024,128]{2,1,0:T(8,128)} %bitcast.5) | data formatting | bytes 1048576
